TPU v7x, 128 devices: a whole 4x4x4 slice. The times are simulated.
128 devices in a mesh: micro: 8 (over y_lo, z), grid: 16 (over y_hi, x, core).
Axes of the slice: x: 4, y: 4 (y_hi: 2, y_lo: 2; y = y_hi * 2 + y_lo), z: 4, core: 2. Of those that a mesh axis runs over, the one named last changes fastest.
Arguments:
- orbitals: float32 [2, 64, 64, 16, 256], P(None, 'micro', None, 'grid'), may hold values from -14 to 14
- local_potential: float32 [64, 16, 256], P('micro', 'grid'), may hold values from -1 to 1
- projectors: float32 [2, 32, 16, 256], P(None, None, 'grid'), may hold values from -0.09375 to 0.09375
- strengths: float32 [2, 32], replicated, may hold values from 1 to 12
- material: int32 [64], replicated, may hold values from 0 to 1
- proj_kind: int32 [64], replicated, may hold values from 0 to 1
- point_cell: int32 [64], replicated, may hold values from 0 to 1999
- vector_now: float32 [2000], replicated, may hold values from -3 to 3
- vector_old: float32 [2000], replicated, may hold values from -3 to 3
Outputs:
- orbitals_out: float32 [2, 64, 64, 16, 256], P(None, 'micro', None, 'grid')
- vector_field: float32 [2000], replicated
All inputs are finite; a program needn't handle non-finite values.
Results may differ from a plain program's by a relative error of at most 0.0003.
Values sent between devices are 32-bit elements; how exact they have to be, the bound alone decides.
No kernel may reach another device: no remote copies, remote signals or barrier semaphores. Data moves between devices by JAX's collectives and lax.ppermute only.
A program may use at most 128 MiB of HBM per device.

v0:
```python
import functools

import jax
import jax.numpy as jnp
from jax import lax
from jax.experimental import pallas as pl
from jax.experimental.pallas import tpu as pltpu
from jax.sharding import PartitionSpec as P

ORB = 64
STEPS = 2
ORDER = 4
SPACING = 0.64
TIME_STEP = 0.05
COURANT = 0.9
COUPLING = 1.0

GRID = 16
LOCAL = 8
HALF = 32
CELLS = 4096
NPROJ = 32
LANES = 128
WIDTH = 2 * LANES
PAYLOAD = 200
MACRO_ROWS = 16
KINETIC = TIME_STEP / (2.0 * SPACING**2)
F32 = jnp.float32
BF16 = jnp.bfloat16
VMEM = pl.BlockSpec(memory_space=pltpu.VMEM)
SMEM = pl.BlockSpec(memory_space=pltpu.SMEM)


def split(value):
    high = value.astype(BF16)
    low = (value - high.astype(F32)).astype(BF16)
    return high, low


def dot(a, b):
    return jnp.dot(a, b, preferred_element_type=F32)


def pack_kernel(kind_ref, x_ref, proj_ref, pot_ref, out_ref):
    first = lax.axis_index("micro") * LOCAL
    for p in range(LOCAL):
        kind = kind_ref[first + p]
        for h in range(2):
            g = 2 * p + h
            for half in range(2):
                for ri in range(2):
                    row = half * 64 + ri * 32
                    out_ref[g, row : row + 32, :] = x_ref[ri, p, h, pl.ds(half, 32, stride=2), :]
                row = 128 + half * 32
                out_ref[g, row : row + 32, :] = proj_ref[kind, pl.ds(half, 32, stride=2), :]
            out_ref[g, 192:200, :] = jnp.broadcast_to(pot_ref[2 * p : 2 * p + 1, :], (8, LANES))
            out_ref[g, 193:194, :] = pot_ref[2 * p + 1 : 2 * p + 2, :]


def turned(block, turn_ref, slot):
    turn_ref[slot] = block.T
    even = turn_ref[slot, pl.ds(0, 64, stride=2), :].reshape(8, 8, LANES)
    odd = turn_ref[slot, pl.ds(1, 64, stride=2), :].reshape(8, 8, LANES)
    return jnp.concatenate([even, odd], axis=1)


def unpack(recv_ref, term_ref, sum_ref, pieces_ref, diag_ref, beta_ref, rows_ref, columns_ref, turn_ref):
    for x in range(4):
        for half in range(2):
            y = pl.ds(half * 8, 8)
            for ri in range(2):
                row = half * 64 + ri * 32
                block = jnp.concatenate([recv_ref[4 * k + x, row : row + 32, :] for k in range(4)], axis=0)
                tile = turned(block, turn_ref, ri)
                term_ref[0, ri, y, x] = tile
                sum_ref[ri, y, x] = tile
                high, low = split(tile)
                lanes = slice(ri * LANES, (ri + 1) * LANES)
                pieces_ref[0, y, x, :, lanes] = high
                pieces_ref[1, y, x, :, lanes] = low
            row = 192 + half
            block = jnp.concatenate(
                [jnp.broadcast_to(recv_ref[4 * k + x, row : row + 1, :], (32, LANES)) for k in range(4)], axis=0
            )
            diag_ref[y, x] = TIME_STEP * (3.0 / SPACING**2 + turned(block, turn_ref, 2))
            row = 128 + half * 32
            block = jnp.concatenate([recv_ref[4 * k + x, row : row + 32, :] for k in range(4)], axis=0)
            tile = turned(block, turn_ref, 3)
            beta_ref[y, x] = tile
            high, low = split(tile)
            rows_ref[y, x, :, 0:128] = high
            rows_ref[y, x, :, 128:256] = low
            rows_ref[y, x, :, 256:384] = high
    for b in range(8):
        block = beta_ref[2 * b : 2 * b + 2].reshape(LANES, LANES).T
        high, low = split(block)
        columns_ref[0:128, b * LANES : (b + 1) * LANES] = high
        columns_ref[128:256, b * LANES : (b + 1) * LANES] = low


def propagate(a, weight, term_ref, sum_ref, pieces_ref, diag_ref, rows_ref, columns_ref, nonlocal_ref, coef_ref):
    diag_shift = TIME_STEP * 0.5 * a * a
    drift = a * (TIME_STEP / (2.0 * SPACING))
    group_of_lane = lax.broadcasted_iota(jnp.int32, (NPROJ, WIDTH), 1) % LANES // 32

    def order(n, _):
        now = (n + 1) % 2
        later = n % 2
        scale = jnp.where(n == 1, 1.0, jnp.where(n == 2, 1.0 / 2, jnp.where(n == 3, 1.0 / 3, 1.0 / 4))).astype(F32)
        high = pieces_ref[0].reshape(1024, WIDTH)
        low = pieces_ref[1].reshape(1024, WIDTH)
        both = dot(columns_ref[...], high)
        coef = both[0:128] + both[128:256] + dot(columns_ref[0:128], low)
        mine = jnp.zeros((NPROJ, WIDTH), F32)
        for k in range(4):
            mine = mine + jnp.where(group_of_lane == k, coef[k * 32 : k * 32 + 32], 0.0)
        parts = []
        for ri in range(2):
            part = mine[:, ri * LANES : (ri + 1) * LANES]
            part = part + pltpu.roll(part, 64, 1)
            part = part + pltpu.roll(part, 32, 1)
            parts.append(part)
        mine = jnp.concatenate(parts, axis=1) * weight
        for k in range(4):
            high, low = split(jnp.where(group_of_lane == k, mine, 0.0))
            coef_ref[k * 32 : k * 32 + 32, :] = high
            coef_ref[128 + k * 32 : 128 + k * 32 + 32, :] = high
            coef_ref[256 + k * 32 : 256 + k * 32 + 32, :] = low
        nonlocal_ref[...] = dot(rows_ref[...].reshape(1024, 384), coef_ref[...]).reshape(16, 4, 16, WIDTH)

        def row(y, _):
            above = (y + 1) % 16
            below = (y + 15) % 16
            centre = [[term_ref[now, ri, y, x] for x in range(4)] for ri in range(2)]
            for x in range(4):
                diag = diag_ref[y, x] + diag_shift
                kinetic, gradient = [], []
                for ri in range(2):
                    c = centre[ri][x]
                    right = centre[ri][x + 1] if x < 3 else pltpu.roll(centre[ri][0], 96, 1)
                    left = centre[ri][x - 1] if x > 0 else pltpu.roll(centre[ri][3], 32, 1)
                    across = right + left + (term_ref[now, ri, above, x] + term_ref[now, ri, below, x])
                    even, odd = c[0:8], c[8:16]
                    before = pltpu.roll(odd, 1, 0)
                    after = pltpu.roll(even, 7, 0)
                    around = across + jnp.concatenate([odd + before, after + even], axis=0)
                    gradient.append(jnp.concatenate([odd - before, after - even], axis=0))
                    there = nonlocal_ref[y, x, :, ri * LANES : (ri + 1) * LANES]
                    kinetic.append(diag * c - KINETIC * around + there)
                new = [
                    scale * (kinetic[1] - drift * gradient[0]),
                    scale * (-kinetic[0] - drift * gradient[1]),
                ]
                for ri in range(2):
                    term_ref[later, ri, y, x] = new[ri]
                    sum_ref[ri, y, x] = sum_ref[ri, y, x] + new[ri]
                    high, low = split(new[ri])
                    lanes = slice(ri * LANES, (ri + 1) * LANES)
                    pieces_ref[0, y, x, :, lanes] = high
                    pieces_ref[1, y, x, :, lanes] = low
            return 0

        lax.fori_loop(0, 16, row, 0)
        return 0

    lax.fori_loop(1, ORDER + 1, order, 0)


def partial_current(a, sum_ref):
    def row(y, total):
        for x in range(4):
            real, imag = sum_ref[0, y, x], sum_ref[1, y, x]
            real_even, real_odd = real[0:8], real[8:16]
            imag_even, imag_odd = imag[0:8], imag[8:16]
            flow = real_even * imag_odd - imag_even * real_odd
            flow = flow + (real_odd * pltpu.roll(imag_even, 7, 0) - imag_odd * pltpu.roll(real_even, 7, 0))
            square = real * real + imag * imag
            total = total + (flow * (1.0 / SPACING) + a * (square[0:8] + square[8:16]))
        return total

    total = lax.fori_loop(0, 16, row, jnp.zeros((8, LANES), F32))
    total = jnp.sum(jnp.sum(total, axis=0, keepdims=True), axis=1, keepdims=True)
    return total * (2.0 / (ORB * CELLS))


def my_point():
    return lax.axis_index("micro") * LOCAL + lax.axis_index("grid") // 2


def is_occupied(material_ref):
    return jnp.logical_or(lax.axis_index("grid") % 2 == 0, material_ref[my_point()] == 1)


def projector_weight(kind_ref, strength_ref):
    kind = kind_ref[my_point()]
    row = jnp.where(kind == 0, strength_ref[0:1, :], strength_ref[1:2, :])
    across = lax.broadcasted_iota(jnp.int32, (NPROJ, NPROJ), 1)
    down = lax.broadcasted_iota(jnp.int32, (NPROJ, NPROJ), 0)
    return TIME_STEP * jnp.sum(jnp.where(across == down, row, 0.0), axis=1, keepdims=True)


def first_kernel(
    kind_ref, cell_ref, material_ref, vector_ref, strength_ref, recv_ref,
    sum_ref, diag_ref, rows_ref, columns_ref, part_ref,
    term_ref, pieces_ref, beta_ref, turn_ref, nonlocal_ref, coef_ref,
):
    unpack(recv_ref, term_ref, sum_ref, pieces_ref, diag_ref, beta_ref, rows_ref, columns_ref, turn_ref)
    a = vector_ref[cell_ref[my_point()]]
    weight = projector_weight(kind_ref, strength_ref)
    propagate(a, weight, term_ref, sum_ref, pieces_ref, diag_ref, rows_ref, columns_ref, nonlocal_ref, coef_ref)
    part = jnp.where(is_occupied(material_ref), partial_current(a, sum_ref), 0.0)
    part_ref[...] = jnp.broadcast_to(part, (LANES, LANES))


def macro_index():
    down = lax.broadcasted_iota(jnp.int32, (MACRO_ROWS, LANES), 0)
    return down * LANES + lax.broadcasted_iota(jnp.int32, (MACRO_ROWS, LANES), 1)


def next_vector(cell_ref, gathered_ref, present, previous, cells):
    index = macro_index()
    deposit = jnp.zeros((MACRO_ROWS, LANES), F32)
    for point in range(64):
        current = gathered_ref[2 * point : 2 * point + 1, :] + gathered_ref[2 * point + 1 : 2 * point + 2, :]
        deposit = deposit + jnp.where(index == cell_ref[point], current, 0.0)
    lane = lax.broadcasted_iota(jnp.int32, (MACRO_ROWS, LANES), 1)
    zero_row = jnp.zeros((1, LANES), F32)
    back = pltpu.roll(present, 1, 1)
    back = jnp.where(lane == 0, jnp.concatenate([zero_row, back[:-1]], axis=0), back)
    forth = pltpu.roll(present, LANES - 1, 1)
    forth = jnp.where(lane == LANES - 1, jnp.concatenate([forth[1:], zero_row], axis=0), forth)
    curvature = forth + back - 2.0 * present
    following = 2.0 * present - previous + COURANT**2 * curvature - COUPLING * deposit
    return jnp.where(index < cells, following, 0.0)


def second_kernel(
    cells,
    kind_ref, cell_ref, material_ref, strength_ref, gathered_ref, now_ref, old_ref,
    field_ref, diag_ref, rows_ref, columns_ref,
    out_ref, vector_ref, part_ref,
    term_ref, sum_ref, pieces_ref, turn_ref, nonlocal_ref, coef_ref,
):
    following = next_vector(cell_ref, gathered_ref, now_ref[...], old_ref[...], cells)
    vector_ref[...] = following
    mine = jnp.where(macro_index() == cell_ref[my_point()], following, 0.0)
    a = jnp.sum(jnp.sum(mine, axis=0, keepdims=True), axis=1, keepdims=True)
    weight = projector_weight(kind_ref, strength_ref)
    for ri in range(2):
        for x in range(4):
            tile = field_ref[ri, :, x]
            term_ref[0, ri, :, x] = tile
            sum_ref[ri, :, x] = tile
            high, low = split(tile)
            lanes = slice(ri * LANES, (ri + 1) * LANES)
            pieces_ref[0, :, x, :, lanes] = high
            pieces_ref[1, :, x, :, lanes] = low
    propagate(a, weight, term_ref, sum_ref, pieces_ref, diag_ref, rows_ref, columns_ref, nonlocal_ref, coef_ref)
    occupied = is_occupied(material_ref)
    part = jnp.where(occupied, partial_current(a, sum_ref), 0.0)
    part_ref[...] = jnp.broadcast_to(part, (LANES, LANES))
    keep = jnp.where(occupied, 1.0, 0.0).astype(F32)
    for x in range(4):
        for half in range(2):
            for ri in range(2):
                tile = sum_ref[ri, pl.ds(half * 8, 8), x] * keep
                turn_ref[ri, pl.ds(0, 64, stride=2), :] = tile[:, 0:8].reshape(64, LANES)
                turn_ref[ri, pl.ds(1, 64, stride=2), :] = tile[:, 8:16].reshape(64, LANES)
                block = turn_ref[ri].T
                for k in range(4):
                    out_ref[4 * k + x, pl.ds(ri * 64 + half, 32, stride=2), :] = block[k * 32 : k * 32 + 32]


def last_kernel(cells, cell_ref, gathered_ref, now_ref, old_ref, out_ref):
    out_ref[...] = next_vector(cell_ref, gathered_ref, now_ref[...], old_ref[...], cells)


FIELD = (2, 16, 4, 16, LANES)
PARAMS = pltpu.CompilerParams(vmem_limit_bytes=24 * 2**20)


def local(
    orbitals,
    local_potential,
    projectors,
    strengths,
    material,
    proj_kind,
    point_cell,
    vector_now,
    vector_old,
):
    cells = vector_now.shape[0]
    shape = jax.ShapeDtypeStruct
    packed = pl.pallas_call(
        pack_kernel,
        out_shape=shape((GRID, PAYLOAD, LANES), F32),
        in_specs=[SMEM, VMEM, VMEM, VMEM],
        out_specs=VMEM,
        compiler_params=PARAMS,
        name="pack",
    )(
        proj_kind,
        orbitals.reshape(2, LOCAL, 2, 64, LANES),
        projectors.reshape(2, 64, LANES),
        local_potential.reshape(16, LANES),
    )
    received = lax.all_to_all(packed, "grid", split_axis=0, concat_axis=0, tiled=True)
    working = [
        pltpu.VMEM((2,) + FIELD, F32),
        pltpu.VMEM((2, 16, 4, 16, WIDTH), BF16),
        pltpu.VMEM(FIELD[1:], F32),
        pltpu.VMEM((4, LANES, LANES), F32),
        pltpu.VMEM((16, 4, 16, WIDTH), F32),
        pltpu.VMEM((384, WIDTH), BF16),
    ]
    field, diag, rows, columns, part = pl.pallas_call(
        first_kernel,
        out_shape=[
            shape(FIELD, F32),
            shape(FIELD[1:], F32),
            shape((16, 4, 16, 384), BF16),
            shape((256, 1024), BF16),
            shape((LANES, LANES), F32),
        ],
        in_specs=[SMEM] * 4 + [VMEM] * 2,
        out_specs=[VMEM] * 5,
        scratch_shapes=working,
        compiler_params=PARAMS,
        name="first",
    )(proj_kind, point_cell, material, vector_now, strengths, received)

    def gather(part):
        part = part.reshape(LANES, 1, LANES)
        part = lax.all_to_all(part, ("micro", "grid"), split_axis=0, concat_axis=0, tiled=True)
        return part.reshape(LANES, LANES)

    macro = MACRO_ROWS * LANES
    now = jnp.pad(vector_now, (0, macro - cells)).reshape(MACRO_ROWS, LANES)
    old = jnp.pad(vector_old, (0, macro - cells)).reshape(MACRO_ROWS, LANES)
    out, following, part = pl.pallas_call(
        functools.partial(second_kernel, cells),
        out_shape=[
            shape((GRID, LANES, LANES), F32),
            shape((MACRO_ROWS, LANES), F32),
            shape((LANES, LANES), F32),
        ],
        in_specs=[SMEM] * 3 + [VMEM] * 8,
        out_specs=[VMEM] * 3,
        scratch_shapes=[working[0], pltpu.VMEM(FIELD, F32), working[1]] + working[3:],
        compiler_params=PARAMS,
        name="second",
    )(proj_kind, point_cell, material, strengths, gather(part), now, old, field, diag, rows, columns)
    out = lax.all_to_all(out, "grid", split_axis=0, concat_axis=0, tiled=True)
    last = pl.pallas_call(
        functools.partial(last_kernel, cells),
        out_shape=shape((MACRO_ROWS, LANES), F32),
        in_specs=[SMEM] + [VMEM] * 3,
        out_specs=VMEM,
        compiler_params=PARAMS,
        name="last",
    )(point_cell, gather(part), following, now)
    out = out.reshape(LOCAL, 2, 2, 64, LANES).transpose(2, 0, 1, 3, 4)
    return out.reshape(orbitals.shape), last.reshape(macro)[:cells]


def solution(mesh):
    in_specs = (
        P(None, "micro", None, "grid", None),
        P("micro", "grid", None),
        P(None, None, "grid", None),
        P(),
        P(),
        P(),
        P(),
        P(),
        P(),
    )
    out_specs = (P(None, "micro", None, "grid", None), P())
    return jax.shard_map(local, mesh=mesh, in_specs=in_specs, out_specs=out_specs, check_vma=False)
```

profile of v0, /device:TPU:0, one launch (start us, length us, event | category | flops | bytes accessed | tf_op | source)
XLA Modules:
  0.0 121.2 jit_solution(16557912028983652533)
XLA Ops:
  0.6 0.0 copy-start
  0.6 1.2 %copy-done = f32[2,8,64,1,256]{4,3,2,1,0:T(1,128)S(1)} copy-done((f32[2,8,64,1,256]{4,3,2,1,0:T(1,128)S(1)}, f32[2,8,64,1,256]{4,3,2,1,0:T(1,128)}, u32[]{:S(2)}) %copy-start) | copy-done | bytes 1048600
  1.9 0.0 copy-start.1
  1.9 0.8 copy-done.1
  2.7 0.0 copy-start.3
  2.7 0.7 copy-done.3
  3.4 0.0 copy-start.4
  3.4 0.7 copy-done.4
  4.0 0.7 pack.1
  4.7 0.0 copy-start.2
  4.7 0.0 copy-start.6
  4.7 0.0 copy-start.7
  4.7 0.0 copy-start.8
  4.8 31.3 %all_to_all.20.recv_ref = f32[16,200,128]{2,1,0:T(8,128)S(1)} all-to-all(f32[16,200,128]{2,1,0:T(8,128)S(1)} %pack.1), channel_id=1, replica_groups=mesh['micro'=8,'grid'=16] {'grid'}, dimensions={0} | all-to-all | bytes 3276800 | tf_op jit(solution)/shard_map/all_to_all | solution.py:308
  36.1 0.0 copy-done.2
  36.1 0.0 copy-done.6
  36.1 0.0 copy-done.7
  36.1 0.0 copy-done.8
  36.1 0.0 copy-start.9
  36.1 0.0 copy-start.5
  36.1 16.3 %first.1 = (f32[2,16,4,16,128]{4,3,2,1,0:T(8,128)S(1)}, f32[16,4,16,128]{3,2,1,0:T(8,128)S(1)}, bf16[16,4,16,384]{3,2,1,0:T(8,128)(2,1)S(1)}, bf16[256,1024]{1,0:T(8,128)(2,1)S(1)}, f32[128,128]{1,0:T(8,128)}) custom-call(s32[64]{0:T(128)S(1)} %copy-done.4, s32[64]{0:T(128)S(1)} %copy-done.6, s32[64]{0:T(128)S(1)} %copy-done.8, f32[2000]{0:T(1024)S(1)} %copy-done.2, ...), custom_call_target="tpu_custom_call" | custom-call | tf_op jit(solution)/shard_map/first/pallas_call | solution.py:317
  52.5 6.8 %all-to-all-start.1 = ((f32[128,1,128]{2,1,0:T(1,128)}), f32[128,1,128]{2,1,0:T(1,128)S(1)}, u32[]{:S(2)}, u32[]{:S(2)}) async-start(f32[128,1,128]{2,1,0:T(1,128)} %bitcast.4), calls=%async_computation.1 | async-start | bytes 131072 | tf_op jit(solution)/shard_map/all_to_all | solution.py:335
  59.2 0.0 copy-done.9
  59.3 9.2 %all-to-all-done.1 = f32[128,1,128]{2,1,0:T(1,128)S(1)} async-done(((f32[128,1,128]{2,1,0:T(1,128)}), f32[128,1,128]{2,1,0:T(1,128)S(1)}, u32[]{:S(2)}, u32[]{:S(2)}) %all-to-all-start.1) | async-done | bytes 65568 | tf_op jit(solution)/shard_map/all_to_all | solution.py:335
  68.5 0.0 copy-done.5
  68.5 16.3 %second.1 = (f32[16,128,128]{2,1,0:T(8,128)}, f32[16,128]{1,0:T(8,128)S(1)}, f32[128,128]{1,0:T(8,128)S(1)}) custom-call(s32[64]{0:T(128)S(1)} %copy-done.5, s32[64]{0:T(128)S(1)} %copy-done.6, s32[64]{0:T(128)S(1)} %copy-done.8, f32[2,32]{1,0:T(2,128)S(1)} %copy-done.7, f32[128,128]{1,0:T(8,128)S(1)} %bitcast.22, ...), custom_call_target="tpu_custom_call" | custom-call | tf_op jit(solution)/shard_map/second/pallas_call | solution.py:341
  84.7 13.8 %all_to_all.21 = f32[128,1,128]{2,1,0:T(1,128)S(1)} all-to-all(f32[128,1,128]{2,1,0:T(1,128)S(1)} %bitcast.25), channel_id=1, replica_groups=mesh['micro'=8,'grid'=16] {'micro','grid'}, dimensions={0} | all-to-all | bytes 131072 | tf_op jit(solution)/shard_map/all_to_all | solution.py:335
  98.6 3.7 %all-to-all-start.2 = ((f32[16,128,128]{2,1,0:T(8,128)}), f32[16,128,128]{2,1,0:T(8,128)S(1)}, u32[]{:S(2)}, u32[]{:S(2)}) async-start(f32[16,128,128]{2,1,0:T(8,128)} %get-tuple-element.15), calls=%async_computation.2 | async-start | bytes 2097152 | tf_op jit(solution)/shard_map/all_to_all | solution.py:354
  102.2 1.2 %last.1 = f32[16,128]{1,0:T(8,128)} custom-call(s32[64]{0:T(128)S(1)} %copy-done.6, f32[128,128]{1,0:T(8,128)S(1)} %bitcast.23, f32[16,128]{1,0:T(8,128)S(1)} %get-tuple-element.17.now_ref, f32[16,128]{1,0:T(8,128)S(1)} %get-tuple-element.19.now_ref.old_ref), custom_call_target="tpu_custom_call" | custom-call | tf_op jit(solution)/shard_map/last/pallas_call | solution.py:355
  103.5 16.7 %all-to-all-done.2 = f32[16,128,128]{2,1,0:T(8,128)S(1)} async-done(((f32[16,128,128]{2,1,0:T(8,128)}), f32[16,128,128]{2,1,0:T(8,128)S(1)}, u32[]{:S(2)}, u32[]{:S(2)}) %all-to-all-start.2) | async-done | bytes 1048608 | tf_op jit(solution)/shard_map/all_to_all | solution.py:354
  120.2 1.0 copy.13
  (1 shorter events, 0.0 us)
Async XLA Ops:
  0.6 1.2 %copy-start = (f32[2,8,64,1,256]{4,3,2,1,0:T(1,128)S(1)}, f32[2,8,64,1,256]{4,3,2,1,0:T(1,128)}, u32[]{:S(2)}) copy-start(f32[2,8,64,1,256]{4,3,2,1,0:T(1,128)} %param.9) | copy-start | bytes 3145732
  1.9 0.8 copy-start.1
  2.7 0.7 copy-start.3
  3.4 0.7 copy-start.4
  4.7 31.4 %copy-start.2 = (f32[2000]{0:T(1024)S(1)}, f32[2000]{0:T(1024)}, u32[]{:S(2)}) copy-start(f32[2000]{0:T(1024)} %vector_ref.1) | copy-start | bytes 24004
  4.7 31.4 %copy-start.6 = (s32[64]{0:T(128)S(1)}, s32[64]{0:T(128)}, u32[]{:S(2)}) copy-start(s32[64]{0:T(128)} %cell_ref.5) | copy-start | bytes 772
  4.7 31.4 %copy-start.7 = (f32[2,32]{1,0:T(2,128)S(1)}, f32[2,32]{1,0:T(2,128)}, u32[]{:S(2)}) copy-start(f32[2,32]{1,0:T(2,128)} %strength_ref.3) | copy-start | bytes 772
  4.7 31.4 %copy-start.8 = (s32[64]{0:T(128)S(1)}, s32[64]{0:T(128)}, u32[]{:S(2)}) copy-start(s32[64]{0:T(128)} %material_ref.3) | copy-start | bytes 772
  36.1 23.1 %copy-start.9 = (f32[2000]{0:T(1024)S(1)}, f32[2000]{0:T(1024)}, u32[]{:S(2)}) copy-start(f32[2000]{0:T(1024)} %param.17) | copy-start | bytes 24004
  36.1 32.3 %copy-start.5 = (s32[64]{0:T(128)S(1)}, s32[64]{0:T(128)}, u32[]{:S(2)}) copy-start(s32[64]{0:T(128)} %kind_ref.5) | copy-start | bytes 772
  52.5 16.0 %all-to-all-start.1 = ((f32[128,1,128]{2,1,0:T(1,128)}), f32[128,1,128]{2,1,0:T(1,128)S(1)}, u32[]{:S(2)}, u32[]{:S(2)}) async-start(f32[128,1,128]{2,1,0:T(1,128)} %bitcast.4), calls=%async_computation.1 | async-start | bytes 131072 | tf_op jit(solution)/shard_map/all_to_all | solution.py:335
  98.6 21.6 %all-to-all-start.2 = ((f32[16,128,128]{2,1,0:T(8,128)}), f32[16,128,128]{2,1,0:T(8,128)S(1)}, u32[]{:S(2)}, u32[]{:S(2)}) async-start(f32[16,128,128]{2,1,0:T(8,128)} %get-tuple-element.15), calls=%async_computation.2 | async-start | bytes 2097152 | tf_op jit(solution)/shard_map/all_to_all | solution.py:354
where the time goes:
time: 122 us; the launch traced here: 121 us
  blocking collectives  45.2 us (37%)
  Pallas kernels  34.5 us (28%)
  waiting for transfers between devices  25.9 us (21%)
  starting transfers between devices  10.4 us (9%)
  local copies, waits for them, and re-layouts  4.49 us (4%)
    all_to_all x1, blocking collectives, local(): lax.all_to_all(packed, 'grid', split_axis=0, concat_axis=0, tiled=True)  31.3 us
    all_to_all x1, waiting for transfers between devices, local(): out = lax.all_to_all(out, 'grid', split_axis=0, concat_axis=0, tiled=True)  16.7 us
    pallas_call x1, Pallas kernels, local(): pl.pallas_call(first_kernel, out_shape=[shape(FIELD, F32), shape(FIELD[1:...  16.3 us
    pallas_call x1, Pallas kernels, local(): pl.pallas_call(functools.partial(second_kernel, cells), out_shape=[shape(...  16.3 us
    all_to_all x1, blocking collectives, gather(): lax.all_to_all(part, ('micro', 'grid'), split_axis=0, concat_axis=0, tile...  13.8 us
    all_to_all x1, waiting for transfers between devices, gather(): lax.all_to_all(part, ('micro', 'grid'), split_axis=0, concat_axis=0, tile...  9.2 us
    all_to_all x1, starting transfers between devices, gather(): lax.all_to_all(part, ('micro', 'grid'), split_axis=0, concat_axis=0, tile...  6.77 us
    all_to_all x1, starting transfers between devices, local(): out = lax.all_to_all(out, 'grid', split_axis=0, concat_axis=0, tiled=True)  3.66 us
  transfers between devices with their start and end apart: 2, of which 2 were waited for; matrix products, arithmetic and copies ran while one was open for 0% of the time, Pallas kernels for 1%

commit v1 on v0

v1 whole, which is shorter than its diff:
```python
import functools

import jax
import jax.numpy as jnp
from jax import lax
from jax.experimental import pallas as pl
from jax.experimental.pallas import tpu as pltpu
from jax.sharding import PartitionSpec as P

ORB = 64
STEPS = 2
ORDER = 4
SPACING = 0.64
TIME_STEP = 0.05
COURANT = 0.9
COUPLING = 1.0

GRID = 16
LOCAL = 8
HALF = 32
CELLS = 4096
NPROJ = 32
LANES = 128
WIDTH = 2 * LANES
PAYLOAD = 168
RETURN = 136
MACRO_ROWS = 16
KINETIC = TIME_STEP / (2.0 * SPACING**2)
F32 = jnp.float32
BF16 = jnp.bfloat16
VMEM = pl.BlockSpec(memory_space=pltpu.VMEM)
SMEM = pl.BlockSpec(memory_space=pltpu.SMEM)
HBM = pl.BlockSpec(memory_space=pltpu.HBM)


def split(value):
    high = value.astype(BF16)
    low = (value - high.astype(F32)).astype(BF16)
    return high, low


def dot(a, b):
    return jnp.dot(a, b, preferred_element_type=F32)


def pack_kernel(kind_hbm, x_hbm, proj_hbm, pot_hbm, out_ref, kind_ref, pot_ref, small_sem, sem):
    kind_copy = pltpu.make_async_copy(kind_hbm, kind_ref, small_sem.at[0])
    pot_copy = pltpu.make_async_copy(pot_hbm, pot_ref, small_sem.at[1])
    kind_copy.start()
    pot_copy.start()
    copies = []
    for p in range(LOCAL):
        for h in range(2):
            for ri in range(2):
                target = out_ref.at[2 * p + h, pl.ds(ri * 64, 64)]
                copies.append(pltpu.make_async_copy(x_hbm.at[ri, p, h], target, sem.at[len(copies)]))
                copies[-1].start()
    kind_copy.wait()
    first = lax.axis_index("micro") * LOCAL
    for p in range(LOCAL):
        kind = kind_ref[first + p]
        for h in range(2):
            target = out_ref.at[2 * p + h, pl.ds(128, 32)]
            copies.append(pltpu.make_async_copy(proj_hbm.at[kind, pl.ds(h * 32, 32)], target, sem.at[len(copies)]))
            copies[-1].start()
    pot_copy.wait()
    for p in range(LOCAL):
        for h in range(2):
            g = 2 * p + h
            out_ref[g, 160:168, :] = jnp.broadcast_to(pot_ref[2 * p : 2 * p + 1, :], (8, LANES))
            out_ref[g, 161:162, :] = pot_ref[2 * p + 1 : 2 * p + 2, :]
    for copy in copies:
        copy.wait()


def turned(block, turn_ref, slot):
    turn_ref[slot] = block.T
    even = turn_ref[slot, pl.ds(0, 64, stride=2), :].reshape(8, 8, LANES)
    odd = turn_ref[slot, pl.ds(1, 64, stride=2), :].reshape(8, 8, LANES)
    return jnp.concatenate([even, odd], axis=1)


def unpack_kernel(recv_ref, u_ref, pieces_ref, diag_ref, turn_ref):
    for x in range(4):
        for half in range(2):
            y = pl.ds(half * 8, 8)
            for ri in range(2):
                rows = pl.ds(ri * 64 + half, 32, stride=2)
                block = jnp.concatenate([recv_ref[4 * k + x, rows, :] for k in range(4)], axis=0)
                tile = turned(block, turn_ref, (2 * x + half) % 2 * 3 + ri)
                u_ref[ri, y, x] = tile
                high, low = split(tile)
                lanes = slice(ri * LANES, (ri + 1) * LANES)
                pieces_ref[0, y, x, :, lanes] = high
                pieces_ref[1, y, x, :, lanes] = low
            row = 160 + half
            block = jnp.concatenate(
                [jnp.broadcast_to(recv_ref[4 * k + x, row : row + 1, :], (32, LANES)) for k in range(4)], axis=0
            )
            tile = turned(block, turn_ref, (2 * x + half) % 2 * 3 + 2)
            diag_ref[y, x] = TIME_STEP * (3.0 / SPACING**2 + tile)


def unpack_projectors(recv_ref, other_ref, beta_ref, rows_ref, columns_ref, turn_ref):
    for x in range(4):
        for half in range(2):
            y = pl.ds(half * 8, 8)
            own, other = pl.ds(128 + half, 16, stride=2), pl.ds(half, 16, stride=2)
            block = []
            for k in range(4):
                block += [recv_ref[4 * k + x, own, :], other_ref[4 * k + x, other, :]]
            tile = turned(jnp.concatenate(block, axis=0), turn_ref, 2 * (x % 2) + half)
            beta_ref[y, x] = tile
            high, low = split(tile)
            rows_ref[y, x, :, 0:128] = high
            rows_ref[y, x, :, 128:256] = low
            rows_ref[y, x, :, 256:384] = high
    for b in range(8):
        block = beta_ref[2 * b : 2 * b + 2].reshape(LANES, LANES).T
        high, low = split(block)
        columns_ref[0:128, b * LANES : (b + 1) * LANES] = high
        columns_ref[128:256, b * LANES : (b + 1) * LANES] = low


def apply(scale, a, weight, u_ref, term_ref, out_ref, pieces_in, pieces_out, diag_ref, rows_ref, columns_ref, nonlocal_ref, coef_ref, current):
    diag_shift = TIME_STEP * 0.5 * a * a
    drift = a * (TIME_STEP / (2.0 * SPACING))
    group_of_lane = lax.broadcasted_iota(jnp.int32, (NPROJ, WIDTH), 1) % LANES // 32
    high = pieces_in[0].reshape(1024, WIDTH)
    low = pieces_in[1].reshape(1024, WIDTH)
    both = dot(columns_ref[...], high)
    coef = both[0:128] + both[128:256] + dot(columns_ref[0:128], low)
    mine = jnp.zeros((NPROJ, WIDTH), F32)
    for k in range(4):
        mine = mine + jnp.where(group_of_lane == k, coef[k * 32 : k * 32 + 32], 0.0)
    parts = []
    for ri in range(2):
        part = mine[:, ri * LANES : (ri + 1) * LANES]
        part = part + pltpu.roll(part, 64, 1)
        part = part + pltpu.roll(part, 32, 1)
        parts.append(part)
    mine = jnp.concatenate(parts, axis=1) * weight
    for k in range(4):
        high, low = split(jnp.where(group_of_lane == k, mine, 0.0))
        coef_ref[k * 32 : k * 32 + 32, :] = high
        coef_ref[128 + k * 32 : 128 + k * 32 + 32, :] = high
        coef_ref[256 + k * 32 : 256 + k * 32 + 32, :] = low

    def row(y, total):
        above = (y + 1) % 16
        below = (y + 15) % 16
        centre = [[term_ref[ri, y, x] for x in range(4)] for ri in range(2)]
        for x in range(4):
            diag = diag_ref[y, x] + diag_shift
            kinetic, gradient = [], []
            for ri in range(2):
                c = centre[ri][x]
                right = centre[ri][x + 1] if x < 3 else pltpu.roll(centre[ri][0], 96, 1)
                left = centre[ri][x - 1] if x > 0 else pltpu.roll(centre[ri][3], 32, 1)
                across = right + left + (term_ref[ri, above, x] + term_ref[ri, below, x])
                even, odd = c[0:8], c[8:16]
                before = pltpu.roll(odd, 1, 0)
                after = pltpu.roll(even, 7, 0)
                around = across + jnp.concatenate([odd + before, after + even], axis=0)
                gradient.append(jnp.concatenate([odd - before, after - even], axis=0))
                there = nonlocal_ref[y, x, :, ri * LANES : (ri + 1) * LANES]
                kinetic.append(diag * c - KINETIC * around + there)
            new = [
                u_ref[0, y, x] + scale * (kinetic[1] - drift * gradient[0]),
                u_ref[1, y, x] - scale * (kinetic[0] + drift * gradient[1]),
            ]
            for ri in range(2):
                out_ref[ri, y, x] = new[ri]
                if pieces_out is not None:
                    high, low = split(new[ri])
                    lanes = slice(ri * LANES, (ri + 1) * LANES)
                    pieces_out[0, y, x, :, lanes] = high
                    pieces_out[1, y, x, :, lanes] = low
            if current:
                real, imag = new
                real_even, real_odd = real[0:8], real[8:16]
                imag_even, imag_odd = imag[0:8], imag[8:16]
                flow = real_even * imag_odd - imag_even * real_odd
                flow = flow + (real_odd * pltpu.roll(imag_even, 7, 0) - imag_odd * pltpu.roll(real_even, 7, 0))
                square = real * real + imag * imag
                total = total + (flow * (1.0 / SPACING) + a * (square[0:8] + square[8:16]))
        return total

    for chunk in range(4):
        ys = pl.ds(4 * chunk, 4)
        nonlocal_ref[ys] = dot(rows_ref[ys].reshape(256, 384), coef_ref[...]).reshape(4, 4, 16, WIDTH)
    total = jnp.zeros((8, LANES), F32)
    for y in range(16):
        total = row(y, total)
    if current:
        total = jnp.sum(jnp.sum(total, axis=0, keepdims=True), axis=1, keepdims=True)
        return total * (2.0 / (ORB * CELLS))


def propagate(a, weight, u_ref, out_ref, pieces_first, pieces_last, term_refs, pieces_ref, *others):
    one, two = term_refs
    apply(1.0 / 4, a, weight, u_ref, u_ref, one, pieces_first, pieces_ref, *others, False)
    apply(1.0 / 3, a, weight, u_ref, one, two, pieces_ref, pieces_ref, *others, False)
    apply(1.0 / 2, a, weight, u_ref, two, one, pieces_ref, pieces_ref, *others, False)
    return apply(1.0, a, weight, u_ref, one, out_ref, pieces_ref, pieces_last, *others, True)


def my_point():
    return lax.axis_index("micro") * LOCAL + lax.axis_index("grid") // 2


def is_occupied(material_ref):
    return jnp.logical_or(lax.axis_index("grid") % 2 == 0, material_ref[my_point()] == 1)


def projector_weight(kind_ref, strength_ref):
    kind = kind_ref[my_point()]
    row = jnp.where(kind == 0, strength_ref[0:1, :], strength_ref[1:2, :])
    across = lax.broadcasted_iota(jnp.int32, (NPROJ, NPROJ), 1)
    down = lax.broadcasted_iota(jnp.int32, (NPROJ, NPROJ), 0)
    down = (down + lax.axis_index("grid") % 2 * (NPROJ // 2)) % NPROJ
    return TIME_STEP * jnp.sum(jnp.where(across == down, row, 0.0), axis=1, keepdims=True)


def first_kernel(
    kind_ref, cell_ref, material_ref, vector_ref, strength_ref, recv_ref, other_ref,
    u_ref, pieces_in, diag_ref,
    out_ref, pieces_out, rows_ref, columns_ref, part_ref,
    one_ref, two_ref, pieces_ref, beta_ref, turn_ref, nonlocal_ref, coef_ref,
):
    unpack_projectors(recv_ref, other_ref, beta_ref, rows_ref, columns_ref, turn_ref)
    a = vector_ref[cell_ref[my_point()]]
    weight = projector_weight(kind_ref, strength_ref)
    others = (diag_ref, rows_ref, columns_ref, nonlocal_ref, coef_ref)
    part = propagate(a, weight, u_ref, out_ref, pieces_in, pieces_out, (one_ref, two_ref), pieces_ref, *others)
    part_ref[...] = jnp.broadcast_to(jnp.where(is_occupied(material_ref), part, 0.0), (LANES, LANES))


def macro_index():
    down = lax.broadcasted_iota(jnp.int32, (MACRO_ROWS, LANES), 0)
    return down * LANES + lax.broadcasted_iota(jnp.int32, (MACRO_ROWS, LANES), 1)


def next_vector(cell_ref, current, present, previous, cells):
    index = macro_index()
    deposit = jnp.zeros((MACRO_ROWS, LANES), F32)
    for point in range(64):
        deposit = deposit + jnp.where(index == cell_ref[point], current(point), 0.0)
    lane = lax.broadcasted_iota(jnp.int32, (MACRO_ROWS, LANES), 1)
    zero_row = jnp.zeros((1, LANES), F32)
    back = pltpu.roll(present, 1, 1)
    back = jnp.where(lane == 0, jnp.concatenate([zero_row, back[:-1]], axis=0), back)
    forth = pltpu.roll(present, LANES - 1, 1)
    forth = jnp.where(lane == LANES - 1, jnp.concatenate([forth[1:], zero_row], axis=0), forth)
    curvature = forth + back - 2.0 * present
    following = 2.0 * present - previous + COURANT**2 * curvature - COUPLING * deposit
    return jnp.where(index < cells, following, 0.0)


def second_kernel(
    cells,
    kind_ref, cell_ref, material_ref, strength_ref, gathered_ref, now_ref, old_ref,
    u_ref, pieces_in, diag_ref, rows_ref, columns_ref,
    out_ref, vector_ref,
    sum_ref, one_ref, two_ref, pieces_ref, turn_ref, nonlocal_ref, coef_ref,
):

    def current(point):
        return gathered_ref[2 * point : 2 * point + 1, :] + gathered_ref[2 * point + 1 : 2 * point + 2, :]

    following = next_vector(cell_ref, current, now_ref[...], old_ref[...], cells)
    vector_ref[...] = following
    mine = jnp.where(macro_index() == cell_ref[my_point()], following, 0.0)
    a = jnp.sum(jnp.sum(mine, axis=0, keepdims=True), axis=1, keepdims=True)
    weight = projector_weight(kind_ref, strength_ref)
    others = (diag_ref, rows_ref, columns_ref, nonlocal_ref, coef_ref)
    part = propagate(a, weight, u_ref, sum_ref, pieces_in, None, (one_ref, two_ref), pieces_ref, *others)
    occupied = is_occupied(material_ref)
    out_ref[:, 128:136, :] = jnp.broadcast_to(jnp.where(occupied, part, 0.0), (GRID, 8, LANES))
    keep = jnp.where(occupied, 1.0, 0.0).astype(F32)
    for x in range(4):
        for half in range(2):
            for ri in range(2):
                tile = sum_ref[ri, pl.ds(half * 8, 8), x] * keep
                slot = 2 * (x % 2) + ri
                turn_ref[slot, pl.ds(0, 64, stride=2), :] = tile[:, 0:8].reshape(64, LANES)
                turn_ref[slot, pl.ds(1, 64, stride=2), :] = tile[:, 8:16].reshape(64, LANES)
                block = turn_ref[slot].T
                for k in range(4):
                    out_ref[4 * k + x, pl.ds(ri * 64 + half, 32, stride=2), :] = block[k * 32 : k * 32 + 32]


def last_kernel(cells, cell_ref, gathered_ref, now_ref, old_ref, out_ref):
    def current(point):
        return gathered_ref[point : point + 1, :]

    out_ref[...] = next_vector(cell_ref, current, now_ref[...], old_ref[...], cells)


FIELD = (2, 16, 4, 16, LANES)
PIECES = (2, 16, 4, 16, WIDTH)
PARAMS = pltpu.CompilerParams(vmem_limit_bytes=24 * 2**20)


def local(
    orbitals,
    local_potential,
    projectors,
    strengths,
    material,
    proj_kind,
    point_cell,
    vector_now,
    vector_old,
):
    cells = vector_now.shape[0]
    shape = jax.ShapeDtypeStruct
    packed = pl.pallas_call(
        pack_kernel,
        out_shape=shape((GRID, PAYLOAD, LANES), F32),
        in_specs=[HBM] * 4,
        out_specs=VMEM,
        scratch_shapes=[
            pltpu.SMEM(proj_kind.shape, jnp.int32),
            pltpu.VMEM((16, LANES), F32),
            pltpu.SemaphoreType.DMA((2,)),
            pltpu.SemaphoreType.DMA((6 * LOCAL,)),
        ],
        compiler_params=PARAMS,
        name="pack",
    )(
        proj_kind,
        orbitals.reshape(2, LOCAL, 2, 64, LANES),
        projectors.reshape(2, 64, LANES),
        local_potential.reshape(16, LANES),
    )
    received = lax.all_to_all(packed, "grid", split_axis=0, concat_axis=0, tiled=True)
    other = lax.ppermute(received[:, 128:160], "grid", [(i, i ^ 1) for i in range(GRID)])
    field, pieces, diag = pl.pallas_call(
        unpack_kernel,
        out_shape=[shape(FIELD, F32), shape(PIECES, BF16), shape(FIELD[1:], F32)],
        in_specs=[VMEM],
        out_specs=[VMEM] * 3,
        scratch_shapes=[pltpu.VMEM((6, LANES, LANES), F32)],
        compiler_params=PARAMS,
        cost_estimate=pl.CostEstimate(flops=10**7, bytes_accessed=5 * 2**20, transcendentals=0),
        name="unpack",
    )(received)
    fields = [pltpu.VMEM(FIELD, F32)] * 2 + [pltpu.VMEM(PIECES, BF16)]
    working = [
        pltpu.VMEM((4, LANES, LANES), F32),
        pltpu.VMEM((16, 4, 16, WIDTH), F32),
        pltpu.VMEM((384, WIDTH), BF16),
    ]
    field, pieces, rows, columns, part = pl.pallas_call(
        first_kernel,
        out_shape=[
            shape(FIELD, F32),
            shape(PIECES, BF16),
            shape((16, 4, 16, 384), BF16),
            shape((256, 1024), BF16),
            shape((LANES, LANES), F32),
        ],
        in_specs=[SMEM] * 4 + [VMEM] * 6,
        out_specs=[VMEM] * 5,
        scratch_shapes=fields + [pltpu.VMEM(FIELD[1:], F32)] + working,
        compiler_params=PARAMS,
        name="first",
    )(proj_kind, point_cell, material, vector_now, strengths, received, other, field, pieces, diag)
    part = part.reshape(LANES, 1, LANES)
    part = lax.all_to_all(part, ("micro", "grid"), split_axis=0, concat_axis=0, tiled=True)
    macro = MACRO_ROWS * LANES
    now = jnp.pad(vector_now, (0, macro - cells)).reshape(MACRO_ROWS, LANES)
    old = jnp.pad(vector_old, (0, macro - cells)).reshape(MACRO_ROWS, LANES)
    out, following = pl.pallas_call(
        functools.partial(second_kernel, cells),
        out_shape=[shape((GRID, RETURN, LANES), F32), shape((MACRO_ROWS, LANES), F32)],
        in_specs=[SMEM] * 3 + [VMEM] * 9,
        out_specs=[VMEM] * 2,
        scratch_shapes=[pltpu.VMEM(FIELD, F32)] + fields + working,
        compiler_params=PARAMS,
        name="second",
    )(
        proj_kind, point_cell, material, strengths, part.reshape(LANES, LANES), now, old,
        field, pieces, diag, rows, columns,
    )
    out = lax.all_to_all(out, "grid", split_axis=0, concat_axis=0, tiled=True)
    part = jnp.sum(out[:, 128].reshape(LOCAL, 2, LANES), axis=1)
    part = lax.all_to_all(jnp.broadcast_to(part, (8, LOCAL, LANES)), "micro", split_axis=0, concat_axis=0, tiled=True)
    last = pl.pallas_call(
        functools.partial(last_kernel, cells),
        out_shape=shape((MACRO_ROWS, LANES), F32),
        in_specs=[SMEM] + [VMEM] * 3,
        out_specs=VMEM,
        compiler_params=PARAMS,
        name="last",
    )(point_cell, part.reshape(64, LANES), following, now)
    out = out[:, 0:128].reshape(LOCAL, 2, 2, 64, LANES).transpose(2, 0, 1, 3, 4)
    return out.reshape(orbitals.shape), last.reshape(macro)[:cells]


def solution(mesh):
    in_specs = (
        P(None, "micro", None, "grid", None),
        P("micro", "grid", None),
        P(None, None, "grid", None),
        P(),
        P(),
        P(),
        P(),
        P(),
        P(),
    )
    out_specs = (P(None, "micro", None, "grid", None), P())
    return jax.shard_map(local, mesh=mesh, in_specs=in_specs, out_specs=out_specs, check_vma=False)
```

time: 122 us -> 101 us (0.83)
  Pallas kernels: 34.5 us -> 17.9 us
  waiting for transfers between devices: 25.9 us -> 15 us
  blocking collectives: 45.2 us -> 49.9 us
  local copies, waits for them, and re-layouts: 4.49 us -> 7.06 us
    all_to_all x2, waiting for transfers between devices: 25.9 us -> 14.1 us  [the longest x1 9.08 us: local(): lax.all_to_all(part, ('micro', 'grid'), split_axis=0, concat_axis=0, tile...]
    pallas_call x1, Pallas kernels: 16.3 us -> 6.3 us  [local(): pl.pallas_call(functools.partial(second_kernel, cells), out_shape=[shape(...]
    pallas_call x1 -> x2, Pallas kernels: 16.3 us -> 8.12 us  [the longest x1 7.49 us: local(): pl.pallas_call(first_kernel, out_shape=[shape(FIELD, F32), shape(PIECES,...]
    all_to_all x1, blocking collectives: 13.8 us -> 21.7 us  [local(): out = lax.all_to_all(out, 'grid', split_axis=0, concat_axis=0, tiled=True)]
    all_to_all x1, blocking collectives: 31.3 us -> 28.2 us  [local(): lax.all_to_all(packed, 'grid', split_axis=0, concat_axis=0, tiled=True)]
    unnamed x20 -> x24, local copies, waits for them, and re-layouts: 3.45 us -> 5.27 us
    pallas_call x1, Pallas kernels: 0.65 us -> 2.27 us  [local(): pl.pallas_call(pack_kernel, out_shape=shape((GRID, PAYLOAD, LANES), F32),...]
  transfers between devices with their start and end apart: 2 -> 3, of which waited for: 2 -> 3; matrix products, arithmetic and copies ran while one was open for 0% -> 1% of each run, Pallas kernels for 1% -> 1%
where the time goes in v1:
time: 101 us
  blocking collectives  49.9 us (49%)
  Pallas kernels  17.9 us (18%)
  waiting for transfers between devices  15 us (15%)
  starting transfers between devices  10.2 us (10%)
  local copies, waits for them, and re-layouts  7.06 us (7%)
    all_to_all x1, blocking collectives, local(): lax.all_to_all(packed, 'grid', split_axis=0, concat_axis=0, tiled=True)  28.2 us
    all_to_all x1, blocking collectives, local(): out = lax.all_to_all(out, 'grid', split_axis=0, concat_axis=0, tiled=True)  21.7 us
    all_to_all x1, waiting for transfers between devices, local(): lax.all_to_all(part, ('micro', 'grid'), split_axis=0, concat_axis=0, tile...  9.08 us
    pallas_call x1, Pallas kernels, local(): pl.pallas_call(first_kernel, out_shape=[shape(FIELD, F32), shape(PIECES,...  7.49 us
    all_to_all x1, starting transfers between devices, local(): lax.all_to_all(part, ('micro', 'grid'), split_axis=0, concat_axis=0, tile...  6.79 us
    pallas_call x1, Pallas kernels, local(): pl.pallas_call(functools.partial(second_kernel, cells), out_shape=[shape(...  6.3 us
    unnamed x24, local copies, waits for them, and re-layouts  5.27 us
    all_to_all x1, waiting for transfers between devices, local(): lax.all_to_all(jnp.broadcast_to(part, (8, LOCAL, LANES)), 'micro', split_...  5.04 us
  transfers between devices with their start and end apart: 3, of which 3 were waited for; matrix products, arithmetic and copies ran while one was open for 1% of the time, Pallas kernels for 1%

profile of v1, /device:TPU:0, one launch (start us, length us, event | category | flops | bytes accessed | tf_op | source)
XLA Modules:
  0.0 100.8 jit_solution(12796215429749063029)
XLA Ops:
  0.6 0.0 copy-start
  0.6 1.2 %copy-done = f32[2,8,64,1,256]{4,3,2,1,0:T(1,128)S(1)} copy-done((f32[2,8,64,1,256]{4,3,2,1,0:T(1,128)S(1)}, f32[2,8,64,1,256]{4,3,2,1,0:T(1,128)}, u32[]{:S(2)}) %copy-start) | copy-done | bytes 1048600
  1.9 0.0 copy-start.3
  1.9 0.8 copy-done.3
  2.7 0.0 copy-start.5
  2.7 0.7 copy-done.5
  3.4 0.0 copy-start.7
  3.4 0.7 copy-done.7
  4.0 2.3 %pack.1 = f32[16,168,128]{2,1,0:T(8,128)S(1)} custom-call(s32[64]{0:T(128)S(1)} %copy-done.7, f32[2,8,2,64,128]{4,3,2,1,0:T(8,128)S(1)} %bitcast.19, f32[2,64,128]{2,1,0:T(8,128)S(1)} %bitcast.22, f32[16,128]{1,0:T(8,128)S(1)} %bitcast.23), custom_call_target="tpu_custom_call" | custom-call | tf_op jit(solution)/shard_map/pack/pallas_call | solution.py:318
  6.3 28.2 %all_to_all.20.recv_ref = f32[16,168,128]{2,1,0:T(8,128)S(1)} all-to-all(f32[16,168,128]{2,1,0:T(8,128)S(1)} %pack.1), channel_id=1, replica_groups=mesh['micro'=8,'grid'=16] {'grid'}, dimensions={0} | all-to-all | bytes 2752512 | tf_op jit(solution)/shard_map/all_to_all | solution.py:337
  34.5 0.0 copy-start.4
  34.5 0.0 copy-start.6
  34.5 0.0 copy-start.9
  34.5 0.0 copy-start.10
  34.6 0.1 collective-permute-start
  34.7 0.6 unpack.1
  35.3 0.9 collective-permute-done.other_ref
  36.2 0.0 copy-done.4
  36.2 0.0 copy-done.6
  36.2 0.0 copy-done.9
  36.2 0.0 copy-done.10
  36.2 0.0 copy-start.11
  36.2 0.0 copy-start.8
  36.2 7.5 %first.1 = (f32[2,16,4,16,128]{4,3,2,1,0:T(8,128)S(1)}, bf16[2,16,4,16,256]{4,3,2,1,0:T(8,128)(2,1)S(1)}, bf16[16,4,16,384]{3,2,1,0:T(8,128)(2,1)S(1)}, bf16[256,1024]{1,0:T(8,128)(2,1)S(1)}, f32[128,128]{1,0:T(8,128)}) custom-call(s32[64]{0:T(128)S(1)} %copy-done.7, s32[64]{0:T(128)S(1)} %copy-done.6, s32[64]{0:T(128)S(1)} %copy-done.10, ...), custom_call_target="tpu_custom_call" | custom-call | tf_op jit(solution)/shard_map/first/pallas_call | solution.py:355
  43.7 0.0 copy-start.1
  43.7 0.8 copy-done.1
  44.5 6.8 %all-to-all-start.1 = ((f32[128,1,128]{2,1,0:T(1,128)}), f32[128,1,128]{2,1,0:T(1,128)S(1)}, u32[]{:S(2)}, u32[]{:S(2)}) async-start(f32[128,1,128]{2,1,0:T(1,128)} %bitcast.4), calls=%async_computation.1 | async-start | bytes 131072 | tf_op jit(solution)/shard_map/all_to_all | solution.py:371
  51.3 0.0 copy-done.11
  51.3 9.1 %all-to-all-done.1 = f32[128,1,128]{2,1,0:T(1,128)S(1)} async-done(((f32[128,1,128]{2,1,0:T(1,128)}), f32[128,1,128]{2,1,0:T(1,128)S(1)}, u32[]{:S(2)}, u32[]{:S(2)}) %all-to-all-start.1) | async-done | bytes 65568 | tf_op jit(solution)/shard_map/all_to_all | solution.py:371
  60.4 0.0 copy-done.8
  60.4 0.0 copy-start.2
  60.4 1.0 %copy-done.2 = bf16[256,1024]{1,0:T(8,128)(2,1)S(1)} copy-done((bf16[256,1024]{1,0:T(8,128)(2,1)S(1)}, bf16[256,1024]{1,0:T(8,128)(2,1)}, u32[]{:S(2)}) %copy-start.2) | copy-done | bytes 524312
  61.5 6.3 %second.1 = (f32[16,136,128]{2,1,0:T(8,128)S(1)}, f32[16,128]{1,0:T(8,128)S(1)}) custom-call(s32[64]{0:T(128)S(1)} %copy-done.8, s32[64]{0:T(128)S(1)} %copy-done.6, s32[64]{0:T(128)S(1)} %copy-done.10, f32[2,32]{1,0:T(2,128)S(1)} %copy-done.9, f32[128,128]{1,0:T(8,128)S(1)} %bitcast.20, f32[16,128]{1,0:T(8,128)S(1)} %get-tuple-element.23.now_ref.old_ref, ...), custom_call_target="tpu_custom_call" | custom-call | tf_op jit(solution)/shard_map/second/pallas_call | solution.py:375
  67.7 21.7 %all_to_all.21 = f32[16,136,128]{2,1,0:T(8,128)S(1)} all-to-all(f32[16,136,128]{2,1,0:T(8,128)S(1)} %get-tuple-element.20), channel_id=1, replica_groups=mesh['micro'=8,'grid'=16] {'grid'}, dimensions={0} | all-to-all | bytes 2228224 | tf_op jit(solution)/shard_map/all_to_all | solution.py:387
  89.5 0.6 broadcast_in_dim.3
  90.1 3.3 %all-to-all-start.3 = ((f32[8,8,128]{2,1,0:T(8,128)}), f32[8,8,128]{2,1,0:T(8,128)S(1)}, u32[]{:S(2)}, u32[]{:S(2)}) async-start(f32[8,8,128]{2,1,0:T(8,128)} %broadcast_in_dim.3), calls=%async_computation.3 | async-start | bytes 65536 | tf_op jit(solution)/shard_map/all_to_all | solution.py:389
  93.4 0.1 slice.17
  93.5 1.0 %copy.13 = f32[2,8,2,64,128]{4,3,2,1,0:T(8,128)} copy(f32[2,8,2,64,128]{4,3,0,2,1:T(8,128)S(1)} %bitcast.24) | data formatting | bytes 2097152 | tf_op jit(solution)/shard_map/transpose | solution.py:398
  94.6 5.0 %all-to-all-done.3 = f32[8,8,128]{2,1,0:T(8,128)S(1)} async-done(((f32[8,8,128]{2,1,0:T(8,128)}), f32[8,8,128]{2,1,0:T(8,128)S(1)}, u32[]{:S(2)}, u32[]{:S(2)}) %all-to-all-start.3) | async-done | bytes 32800 | tf_op jit(solution)/shard_map/all_to_all | solution.py:389
  99.6 1.2 %last.1 = f32[16,128]{1,0:T(8,128)} custom-call(s32[64]{0:T(128)S(1)} %copy-done.6, f32[64,128]{1,0:T(8,128)S(1)} %bitcast.21, f32[16,128]{1,0:T(8,128)S(1)} %get-tuple-element.21.now_ref, f32[16,128]{1,0:T(8,128)S(1)} %get-tuple-element.23.now_ref.old_ref), custom_call_target="tpu_custom_call" | custom-call | tf_op jit(solution)/shard_map/last/pallas_call | solution.py:390
  (4 shorter events, 0.0 us)
Async XLA Ops:
  0.6 1.2 %copy-start = (f32[2,8,64,1,256]{4,3,2,1,0:T(1,128)S(1)}, f32[2,8,64,1,256]{4,3,2,1,0:T(1,128)}, u32[]{:S(2)}) copy-start(f32[2,8,64,1,256]{4,3,2,1,0:T(1,128)} %param.9) | copy-start | bytes 3145732
  1.9 0.8 copy-start.3
  2.7 0.7 copy-start.5
  3.4 0.7 copy-start.7
  34.5 1.7 %copy-start.4 = (f32[2000]{0:T(1024)S(1)}, f32[2000]{0:T(1024)}, u32[]{:S(2)}) copy-start(f32[2000]{0:T(1024)} %vector_ref.1) | copy-start | bytes 24004
  34.5 1.7 %copy-start.6 = (s32[64]{0:T(128)S(1)}, s32[64]{0:T(128)}, u32[]{:S(2)}) copy-start(s32[64]{0:T(128)} %cell_ref.5) | copy-start | bytes 772
  34.5 1.7 %copy-start.9 = (f32[2,32]{1,0:T(2,128)S(1)}, f32[2,32]{1,0:T(2,128)}, u32[]{:S(2)}) copy-start(f32[2,32]{1,0:T(2,128)} %strength_ref.3) | copy-start | bytes 772
  34.5 1.7 %copy-start.10 = (s32[64]{0:T(128)S(1)}, s32[64]{0:T(128)}, u32[]{:S(2)}) copy-start(s32[64]{0:T(128)} %material_ref.3) | copy-start | bytes 772
  34.6 1.6 %collective-permute-start = (f32[16,32,128]{2,1,0:T(8,128)S(1)}, f32[16,32,128]{2,1,0:T(8,128)S(1)}, u32[]{:S(2)}, u32[]{:S(2)}) collective-permute-start(f32[16,32,128]{2,1,0:T(8,128)S(1)} %slice.16), channel_id=1, source_target_pairs={{0,1},{1,0},{2,3},{3,2},{4,5},{5,4},{6,7},{7,6},{8,9},{9,8},{10,11... | collective-permute-start | bytes 786440 | tf_op jit(solution)/shard_map/ppermute | solution.py:338
  36.2 15.1 %copy-start.11 = (f32[2000]{0:T(1024)S(1)}, f32[2000]{0:T(1024)}, u32[]{:S(2)}) copy-start(f32[2000]{0:T(1024)} %param.17) | copy-start | bytes 24004
  36.2 24.2 %copy-start.8 = (s32[64]{0:T(128)S(1)}, s32[64]{0:T(128)}, u32[]{:S(2)}) copy-start(s32[64]{0:T(128)} %kind_ref.3) | copy-start | bytes 772
  43.7 0.8 copy-start.1
  44.5 15.9 %all-to-all-start.1 = ((f32[128,1,128]{2,1,0:T(1,128)}), f32[128,1,128]{2,1,0:T(1,128)S(1)}, u32[]{:S(2)}, u32[]{:S(2)}) async-start(f32[128,1,128]{2,1,0:T(1,128)} %bitcast.4), calls=%async_computation.1 | async-start | bytes 131072 | tf_op jit(solution)/shard_map/all_to_all | solution.py:371
  60.4 1.0 %copy-start.2 = (bf16[256,1024]{1,0:T(8,128)(2,1)S(1)}, bf16[256,1024]{1,0:T(8,128)(2,1)}, u32[]{:S(2)}) copy-start(bf16[256,1024]{1,0:T(8,128)(2,1)} %copy-done.1) | copy-start | bytes 1572868
  90.1 9.5 %all-to-all-start.3 = ((f32[8,8,128]{2,1,0:T(8,128)}), f32[8,8,128]{2,1,0:T(8,128)S(1)}, u32[]{:S(2)}, u32[]{:S(2)}) async-start(f32[8,8,128]{2,1,0:T(8,128)} %broadcast_in_dim.3), calls=%async_computation.3 | async-start | bytes 65536 | tf_op jit(solution)/shard_map/all_to_all | solution.py:389

commit v2 on v1

--- a/solution.py
+++ b/solution.py
@@ -22,8 +22,8 @@
 NPROJ = 32
 LANES = 128
 WIDTH = 2 * LANES
-PAYLOAD = 168
-RETURN = 136
+PAYLOAD = 162
+RETURN = 130
 MACRO_ROWS = 16
 KINETIC = TIME_STEP / (2.0 * SPACING**2)
 F32 = jnp.float32
@@ -43,32 +43,35 @@
     return jnp.dot(a, b, preferred_element_type=F32)
 
 
-def pack_kernel(kind_hbm, x_hbm, proj_hbm, pot_hbm, out_ref, kind_ref, pot_ref, small_sem, sem):
-    kind_copy = pltpu.make_async_copy(kind_hbm, kind_ref, small_sem.at[0])
-    pot_copy = pltpu.make_async_copy(pot_hbm, pot_ref, small_sem.at[1])
+def pack_kernel(kind_hbm, x_hbm, proj_hbm, pot_hbm, out_ref, kind_ref, sem):
+    copies = []
+
+    def start(source, target):
+        copies.append(pltpu.make_async_copy(source, target, sem.at[len(copies)]))
+        copies[-1].start()
+
+    kind_copy = pltpu.make_async_copy(kind_hbm, kind_ref, sem.at[14])
     kind_copy.start()
-    pot_copy.start()
-    copies = []
-    for p in range(LOCAL):
-        for h in range(2):
-            for ri in range(2):
-                target = out_ref.at[2 * p + h, pl.ds(ri * 64, 64)]
-                copies.append(pltpu.make_async_copy(x_hbm.at[ri, p, h], target, sem.at[len(copies)]))
-                copies[-1].start()
+    for ri in range(2):
+        for part in range(2):
+            points = pl.ds(part * 4, 4)
+            start(x_hbm.at[ri, points], out_ref.at[points, :, pl.ds(ri * 32, 32)])
+    for h in range(2):
+        start(pot_hbm, out_ref.at[:, h, 80])
     kind_copy.wait()
     first = lax.axis_index("micro") * LOCAL
     for p in range(LOCAL):
-        kind = kind_ref[first + p]
-        for h in range(2):
-            target = out_ref.at[2 * p + h, pl.ds(128, 32)]
-            copies.append(pltpu.make_async_copy(proj_hbm.at[kind, pl.ds(h * 32, 32)], target, sem.at[len(copies)]))
-            copies[-1].start()
-    pot_copy.wait()
-    for p in range(LOCAL):
-        for h in range(2):
-            g = 2 * p + h
-            out_ref[g, 160:168, :] = jnp.broadcast_to(pot_ref[2 * p : 2 * p + 1, :], (8, LANES))
-            out_ref[g, 161:162, :] = pot_ref[2 * p + 1 : 2 * p + 2, :]
+        start(proj_hbm.at[kind_ref[first + p]], out_ref.at[p, :, pl.ds(64, 16)])
+    for copy in copies:
+        copy.wait()
+
+
+def unpermute_kernel(recv_ref, out_hbm, sem):
+    copies = []
+    for ri in range(2):
+        source = recv_ref.at[:, :, pl.ds(ri * 32, 32)]
+        copies.append(pltpu.make_async_copy(source, out_hbm.at[ri], sem.at[ri]))
+        copies[-1].start()
     for copy in copies:
         copy.wait()
 
@@ -80,23 +83,38 @@
     return jnp.concatenate([even, odd], axis=1)
 
 
-def unpack_kernel(recv_ref, u_ref, pieces_ref, diag_ref, turn_ref):
+def unpack_kernel(
+    kind_ref, cell_ref, material_ref, vector_ref, strength_ref, recv_ref,
+    u_ref, pieces_ref, diag_ref, small_ref, cells_ref, turn_ref,
+):
+    point = lax.axis_index("micro") * LOCAL + lax.axis_index("grid") // 2
+    occupied = jnp.logical_or(lax.axis_index("grid") % 2 == 0, material_ref[point] == 1)
+    small_ref[0:1, :] = jnp.full((1, LANES), vector_ref[cell_ref[point]], F32)
+    small_ref[1:2, :] = jnp.full((1, LANES), jnp.where(occupied, 1.0, 0.0), F32)
+    small_ref[2:8, :] = jnp.full((6, LANES), cell_ref[point].astype(F32), F32)
+    small_ref[8:40, :] = jnp.broadcast_to(projector_weight(kind_ref[point], strength_ref), (NPROJ, LANES))
+    for p in range(64):
+        cells_ref[p : p + 1, :] = jnp.full((1, LANES), cell_ref[p], jnp.int32)
     for x in range(4):
         for half in range(2):
             y = pl.ds(half * 8, 8)
             for ri in range(2):
-                rows = pl.ds(ri * 64 + half, 32, stride=2)
-                block = jnp.concatenate([recv_ref[4 * k + x, rows, :] for k in range(4)], axis=0)
+                block = []
+                for k in range(4):
+                    rows = pl.ds((4 * k + x) * PAYLOAD + ri * 64 + half, 32, stride=2)
+                    block.append(recv_ref[rows, :])
+                block = jnp.concatenate(block, axis=0)
                 tile = turned(block, turn_ref, (2 * x + half) % 2 * 3 + ri)
                 u_ref[ri, y, x] = tile
                 high, low = split(tile)
                 lanes = slice(ri * LANES, (ri + 1) * LANES)
                 pieces_ref[0, y, x, :, lanes] = high
                 pieces_ref[1, y, x, :, lanes] = low
-            row = 160 + half
-            block = jnp.concatenate(
-                [jnp.broadcast_to(recv_ref[4 * k + x, row : row + 1, :], (32, LANES)) for k in range(4)], axis=0
-            )
+            block = []
+            for k in range(4):
+                row = (4 * k + x) * PAYLOAD + 160 + half
+                block.append(jnp.broadcast_to(recv_ref[row : row + 1, :], (32, LANES)))
+            block = jnp.concatenate(block, axis=0)
             tile = turned(block, turn_ref, (2 * x + half) % 2 * 3 + 2)
             diag_ref[y, x] = TIME_STEP * (3.0 / SPACING**2 + tile)
 
@@ -105,10 +123,10 @@
     for x in range(4):
         for half in range(2):
             y = pl.ds(half * 8, 8)
-            own, other = pl.ds(128 + half, 16, stride=2), pl.ds(half, 16, stride=2)
             block = []
             for k in range(4):
-                block += [recv_ref[4 * k + x, own, :], other_ref[4 * k + x, other, :]]
+                block.append(recv_ref[pl.ds((4 * k + x) * PAYLOAD + 128 + half, 16, stride=2), :])
+                block.append(other_ref[pl.ds((4 * k + x) * 32 + half, 16, stride=2), :])
             tile = turned(jnp.concatenate(block, axis=0), turn_ref, 2 * (x % 2) + half)
             beta_ref[y, x] = tile
             high, low = split(tile)
@@ -197,24 +215,15 @@
         return total * (2.0 / (ORB * CELLS))
 
 
-def propagate(a, weight, u_ref, out_ref, pieces_first, pieces_last, term_refs, pieces_ref, *others):
+def propagate(a, weight, u_ref, out_ref, pieces_first, term_refs, pieces_ref, *others):
     one, two = term_refs
     apply(1.0 / 4, a, weight, u_ref, u_ref, one, pieces_first, pieces_ref, *others, False)
     apply(1.0 / 3, a, weight, u_ref, one, two, pieces_ref, pieces_ref, *others, False)
     apply(1.0 / 2, a, weight, u_ref, two, one, pieces_ref, pieces_ref, *others, False)
-    return apply(1.0, a, weight, u_ref, one, out_ref, pieces_ref, pieces_last, *others, True)
-
-
-def my_point():
-    return lax.axis_index("micro") * LOCAL + lax.axis_index("grid") // 2
-
-
-def is_occupied(material_ref):
-    return jnp.logical_or(lax.axis_index("grid") % 2 == 0, material_ref[my_point()] == 1)
-
-
-def projector_weight(kind_ref, strength_ref):
-    kind = kind_ref[my_point()]
+    return apply(1.0, a, weight, u_ref, one, out_ref, pieces_ref, None, *others, True)
+
+
+def projector_weight(kind, strength_ref):
     row = jnp.where(kind == 0, strength_ref[0:1, :], strength_ref[1:2, :])
     across = lax.broadcasted_iota(jnp.int32, (NPROJ, NPROJ), 1)
     down = lax.broadcasted_iota(jnp.int32, (NPROJ, NPROJ), 0)
@@ -222,18 +231,21 @@
     return TIME_STEP * jnp.sum(jnp.where(across == down, row, 0.0), axis=1, keepdims=True)
 
 
+def doubled(weight):
+    return jnp.concatenate([weight, weight], axis=1)
+
+
 def first_kernel(
-    kind_ref, cell_ref, material_ref, vector_ref, strength_ref, recv_ref, other_ref,
-    u_ref, pieces_in, diag_ref,
-    out_ref, pieces_out, rows_ref, columns_ref, part_ref,
+    small_ref, recv_ref, other_ref, u_ref, pieces_in, diag_ref,
+    out_ref, rows_ref, columns_ref, part_ref,
     one_ref, two_ref, pieces_ref, beta_ref, turn_ref, nonlocal_ref, coef_ref,
 ):
     unpack_projectors(recv_ref, other_ref, beta_ref, rows_ref, columns_ref, turn_ref)
-    a = vector_ref[cell_ref[my_point()]]
-    weight = projector_weight(kind_ref, strength_ref)
+    a = small_ref[0:1, :]
+    weight = doubled(small_ref[8:40, :])
     others = (diag_ref, rows_ref, columns_ref, nonlocal_ref, coef_ref)
-    part = propagate(a, weight, u_ref, out_ref, pieces_in, pieces_out, (one_ref, two_ref), pieces_ref, *others)
-    part_ref[...] = jnp.broadcast_to(jnp.where(is_occupied(material_ref), part, 0.0), (LANES, LANES))
+    part = propagate(a, weight, u_ref, out_ref, pieces_in, (one_ref, two_ref), pieces_ref, *others)
+    part_ref[...] = jnp.broadcast_to(part * small_ref[1:2, :], (LANES, LANES))
 
 
 def macro_index():
@@ -241,11 +253,11 @@
     return down * LANES + lax.broadcasted_iota(jnp.int32, (MACRO_ROWS, LANES), 1)
 
 
-def next_vector(cell_ref, current, present, previous, cells):
+def next_vector(cells_ref, current, present, previous, cells):
     index = macro_index()
     deposit = jnp.zeros((MACRO_ROWS, LANES), F32)
     for point in range(64):
-        deposit = deposit + jnp.where(index == cell_ref[point], current(point), 0.0)
+        deposit = deposit + jnp.where(index == cells_ref[point : point + 1, :], current(point), 0.0)
     lane = lax.broadcasted_iota(jnp.int32, (MACRO_ROWS, LANES), 1)
     zero_row = jnp.zeros((1, LANES), F32)
     back = pltpu.roll(present, 1, 1)
@@ -259,25 +271,28 @@
 
 def second_kernel(
     cells,
-    kind_ref, cell_ref, material_ref, strength_ref, gathered_ref, now_ref, old_ref,
-    u_ref, pieces_in, diag_ref, rows_ref, columns_ref,
+    small_ref, cells_ref, gathered_ref, now_ref, old_ref, u_ref, diag_ref, rows_ref, columns_ref,
     out_ref, vector_ref,
     sum_ref, one_ref, two_ref, pieces_ref, turn_ref, nonlocal_ref, coef_ref,
 ):
-
     def current(point):
         return gathered_ref[2 * point : 2 * point + 1, :] + gathered_ref[2 * point + 1 : 2 * point + 2, :]
 
-    following = next_vector(cell_ref, current, now_ref[...], old_ref[...], cells)
+    for ri in range(2):
+        for y in range(16):
+            high, low = split(u_ref[ri, y])
+            pieces_ref[0, y, :, :, ri * LANES : (ri + 1) * LANES] = high
+            pieces_ref[1, y, :, :, ri * LANES : (ri + 1) * LANES] = low
+    following = next_vector(cells_ref, current, now_ref[...], old_ref[...], cells)
     vector_ref[...] = following
-    mine = jnp.where(macro_index() == cell_ref[my_point()], following, 0.0)
+    mine = jnp.where(macro_index().astype(F32) == small_ref[2:3, :], following, 0.0)
     a = jnp.sum(jnp.sum(mine, axis=0, keepdims=True), axis=1, keepdims=True)
-    weight = projector_weight(kind_ref, strength_ref)
+    weight = doubled(small_ref[8:40, :])
     others = (diag_ref, rows_ref, columns_ref, nonlocal_ref, coef_ref)
-    part = propagate(a, weight, u_ref, sum_ref, pieces_in, None, (one_ref, two_ref), pieces_ref, *others)
-    occupied = is_occupied(material_ref)
-    out_ref[:, 128:136, :] = jnp.broadcast_to(jnp.where(occupied, part, 0.0), (GRID, 8, LANES))
-    keep = jnp.where(occupied, 1.0, 0.0).astype(F32)
+    part = propagate(a, weight, u_ref, sum_ref, pieces_ref, (one_ref, two_ref), pieces_ref, *others)
+    keep = small_ref[1:2, :]
+    for g in range(GRID):
+        out_ref[g * RETURN + 128 : (g + 1) * RETURN, :] = jnp.broadcast_to(part * keep, (2, LANES))
     for x in range(4):
         for half in range(2):
             for ri in range(2):
@@ -287,14 +302,15 @@
                 turn_ref[slot, pl.ds(1, 64, stride=2), :] = tile[:, 8:16].reshape(64, LANES)
                 block = turn_ref[slot].T
                 for k in range(4):
-                    out_ref[4 * k + x, pl.ds(ri * 64 + half, 32, stride=2), :] = block[k * 32 : k * 32 + 32]
-
-
-def last_kernel(cells, cell_ref, gathered_ref, now_ref, old_ref, out_ref):
+                    rows = pl.ds((4 * k + x) * RETURN + ri * 64 + half, 32, stride=2)
+                    out_ref[rows, :] = block[k * 32 : k * 32 + 32]
+
+
+def last_kernel(cells, cells_ref, gathered_ref, now_ref, old_ref, out_ref):
     def current(point):
         return gathered_ref[point : point + 1, :]
 
-    out_ref[...] = next_vector(cell_ref, current, now_ref[...], old_ref[...], cells)
+    out_ref[...] = next_vector(cells_ref, current, now_ref[...], old_ref[...], cells)
 
 
 FIELD = (2, 16, 4, 16, LANES)
@@ -315,58 +331,65 @@
 ):
     cells = vector_now.shape[0]
     shape = jax.ShapeDtypeStruct
+
+    def in_hbm(array, *dims):
+        return pltpu.with_memory_space_constraint(array.reshape(dims), pltpu.HBM)
+
     packed = pl.pallas_call(
         pack_kernel,
-        out_shape=shape((GRID, PAYLOAD, LANES), F32),
+        out_shape=shape((LOCAL, 2, PAYLOAD // 2, 2, LANES), F32),
         in_specs=[HBM] * 4,
         out_specs=VMEM,
-        scratch_shapes=[
-            pltpu.SMEM(proj_kind.shape, jnp.int32),
-            pltpu.VMEM((16, LANES), F32),
-            pltpu.SemaphoreType.DMA((2,)),
-            pltpu.SemaphoreType.DMA((6 * LOCAL,)),
-        ],
+        scratch_shapes=[pltpu.SMEM(proj_kind.shape, jnp.int32), pltpu.SemaphoreType.DMA((15,))],
         compiler_params=PARAMS,
         name="pack",
     )(
-        proj_kind,
-        orbitals.reshape(2, LOCAL, 2, 64, LANES),
-        projectors.reshape(2, 64, LANES),
-        local_potential.reshape(16, LANES),
+        in_hbm(proj_kind, 64),
+        in_hbm(orbitals, 2, LOCAL, 2, 32, 2, LANES),
+        in_hbm(projectors, 2, 2, 16, 2, LANES),
+        in_hbm(local_potential, LOCAL, 2, LANES),
     )
+    packed = packed.reshape(GRID, PAYLOAD // 2, 2, LANES)
     received = lax.all_to_all(packed, "grid", split_axis=0, concat_axis=0, tiled=True)
-    other = lax.ppermute(received[:, 128:160], "grid", [(i, i ^ 1) for i in range(GRID)])
-    field, pieces, diag = pl.pallas_call(
+    other = lax.ppermute(received[:, 64:80], "grid", [(i, i ^ 1) for i in range(GRID)])
+    other = other.reshape(GRID * 32, LANES)
+    received = received.reshape(GRID * PAYLOAD, LANES)
+    field, pieces, diag, small, cell_rows = pl.pallas_call(
         unpack_kernel,
-        out_shape=[shape(FIELD, F32), shape(PIECES, BF16), shape(FIELD[1:], F32)],
-        in_specs=[VMEM],
-        out_specs=[VMEM] * 3,
+        out_shape=[
+            shape(FIELD, F32),
+            shape(PIECES, BF16),
+            shape(FIELD[1:], F32),
+            shape((40, LANES), F32),
+            shape((64, LANES), jnp.int32),
+        ],
+        in_specs=[SMEM] * 4 + [VMEM] * 2,
+        out_specs=[VMEM] * 5,
         scratch_shapes=[pltpu.VMEM((6, LANES, LANES), F32)],
         compiler_params=PARAMS,
         cost_estimate=pl.CostEstimate(flops=10**7, bytes_accessed=5 * 2**20, transcendentals=0),
         name="unpack",
-    )(received)
+    )(proj_kind, point_cell, material, vector_now, strengths, received)
     fields = [pltpu.VMEM(FIELD, F32)] * 2 + [pltpu.VMEM(PIECES, BF16)]
     working = [
         pltpu.VMEM((4, LANES, LANES), F32),
         pltpu.VMEM((16, 4, 16, WIDTH), F32),
         pltpu.VMEM((384, WIDTH), BF16),
     ]
-    field, pieces, rows, columns, part = pl.pallas_call(
+    field, rows, columns, part = pl.pallas_call(
         first_kernel,
         out_shape=[
             shape(FIELD, F32),
-            shape(PIECES, BF16),
             shape((16, 4, 16, 384), BF16),
             shape((256, 1024), BF16),
             shape((LANES, LANES), F32),
         ],
-        in_specs=[SMEM] * 4 + [VMEM] * 6,
-        out_specs=[VMEM] * 5,
+        in_specs=[VMEM] * 6,
+        out_specs=[VMEM] * 4,
         scratch_shapes=fields + [pltpu.VMEM(FIELD[1:], F32)] + working,
         compiler_params=PARAMS,
         name="first",
-    )(proj_kind, point_cell, material, vector_now, strengths, received, other, field, pieces, diag)
+    )(small, received, other, field, pieces, diag)
     part = part.reshape(LANES, 1, LANES)
     part = lax.all_to_all(part, ("micro", "grid"), split_axis=0, concat_axis=0, tiled=True)
     macro = MACRO_ROWS * LANES
@@ -374,28 +397,35 @@
     old = jnp.pad(vector_old, (0, macro - cells)).reshape(MACRO_ROWS, LANES)
     out, following = pl.pallas_call(
         functools.partial(second_kernel, cells),
-        out_shape=[shape((GRID, RETURN, LANES), F32), shape((MACRO_ROWS, LANES), F32)],
-        in_specs=[SMEM] * 3 + [VMEM] * 9,
+        out_shape=[shape((GRID * RETURN, LANES), F32), shape((MACRO_ROWS, LANES), F32)],
+        in_specs=[VMEM] * 9,
         out_specs=[VMEM] * 2,
         scratch_shapes=[pltpu.VMEM(FIELD, F32)] + fields + working,
         compiler_params=PARAMS,
         name="second",
-    )(
-        proj_kind, point_cell, material, strengths, part.reshape(LANES, LANES), now, old,
-        field, pieces, diag, rows, columns,
-    )
+    )(small, cell_rows, part.reshape(LANES, LANES), now, old, field, diag, rows, columns)
+    out = out.reshape(GRID, RETURN // 2, 2, LANES)
     out = lax.all_to_all(out, "grid", split_axis=0, concat_axis=0, tiled=True)
-    part = jnp.sum(out[:, 128].reshape(LOCAL, 2, LANES), axis=1)
+    part = jnp.sum(out[:, 64, 0].reshape(LOCAL, 2, LANES), axis=1)
     part = lax.all_to_all(jnp.broadcast_to(part, (8, LOCAL, LANES)), "micro", split_axis=0, concat_axis=0, tiled=True)
+    out = pl.pallas_call(
+        unpermute_kernel,
+        out_shape=pltpu.HBM((2, LOCAL, 2, 32, 2, LANES), F32),
+        in_specs=[VMEM],
+        out_specs=HBM,
+        scratch_shapes=[pltpu.SemaphoreType.DMA((2,))],
+        compiler_params=PARAMS,
+        cost_estimate=pl.CostEstimate(flops=10**6, bytes_accessed=2 * 2**20, transcendentals=0),
+        name="unpermute",
+    )(out.reshape(LOCAL, 2, RETURN // 2, 2, LANES))
     last = pl.pallas_call(
         functools.partial(last_kernel, cells),
         out_shape=shape((MACRO_ROWS, LANES), F32),
-        in_specs=[SMEM] + [VMEM] * 3,
+        in_specs=[VMEM] * 4,
         out_specs=VMEM,
         compiler_params=PARAMS,
         name="last",
-    )(point_cell, part.reshape(64, LANES), following, now)
-    out = out[:, 0:128].reshape(LOCAL, 2, 2, 64, LANES).transpose(2, 0, 1, 3, 4)
+    )(cell_rows, part.reshape(64, LANES), following, now)
     return out.reshape(orbitals.shape), last.reshape(macro)[:cells]
 
 

time: 101 us -> 93 us (0.921)
  local copies, waits for them, and re-layouts: 7.06 us -> 0.68 us
    unnamed x24 -> x12, local copies, waits for them, and re-layouts: 5.27 us -> 0.04 us
    transpose x1 -> x0, local copies, waits for them, and re-layouts: 1.04 us -> none  [local(): out = out[:, 0:128].reshape(LOCAL, 2, 2, 64, LANES).transpose(2, 0, 1, 3, 4)]
    pallas_call x2 -> x3, Pallas kernels: 9.76 us -> 9.43 us  [the longest x1 6.62 us: local(): pl.pallas_call(first_kernel, out_shape=[shape(FIELD, F32), shape((16, 4,...]
  transfers between devices with their start and end apart: 3 -> 3, of which waited for: 3 -> 3; matrix products, arithmetic and copies ran while one was open for 1% -> 0% of each run, Pallas kernels for 1% -> 3%
where the time goes in v2:
time: 93 us; the launch traced here: 92.6 us
  blocking collectives  49.3 us (53%)
  Pallas kernels  17.2 us (18%)
  waiting for transfers between devices  14.5 us (16%)
  starting transfers between devices  10.2 us (11%)
    all_to_all x1, blocking collectives, local(): lax.all_to_all(packed, 'grid', split_axis=0, concat_axis=0, tiled=True)  27.8 us
    all_to_all x1, blocking collectives, local(): out = lax.all_to_all(out, 'grid', split_axis=0, concat_axis=0, tiled=True)  21.4 us
    all_to_all x1, waiting for transfers between devices, local(): lax.all_to_all(part, ('micro', 'grid'), split_axis=0, concat_axis=0, tile...  9.2 us
    all_to_all x1, starting transfers between devices, local(): lax.all_to_all(part, ('micro', 'grid'), split_axis=0, concat_axis=0, tile...  6.78 us
    pallas_call x1, Pallas kernels, local(): pl.pallas_call(first_kernel, out_shape=[shape(FIELD, F32), shape((16, 4,...  6.62 us
    pallas_call x1, Pallas kernels, local(): pl.pallas_call(functools.partial(second_kernel, cells), out_shape=[shape(...  5.73 us
    all_to_all x1, waiting for transfers between devices, local(): lax.all_to_all(jnp.broadcast_to(part, (8, LOCAL, LANES)), 'micro', split_...  5.2 us
    all_to_all x1, starting transfers between devices, local(): lax.all_to_all(jnp.broadcast_to(part, (8, LOCAL, LANES)), 'micro', split_...  3.32 us
  transfers between devices with their start and end apart: 3, of which 3 were waited for; matrix products, arithmetic and copies ran while one was open for 0% of the time, Pallas kernels for 3%

profile of v2, /device:TPU:0, one launch (start us, length us, event | category | flops | bytes accessed | tf_op | source)
XLA Modules:
  0.0 92.6 jit_solution(11350666720698617681)
XLA Ops:
  0.6 1.8 %pack.1 = f32[8,2,81,2,128]{4,3,2,1,0:T(2,128)S(1)} custom-call(s32[64]{0:T(128)} %kind_ref.1, f32[2,8,2,32,2,128]{5,4,3,2,1,0:T(2,128)} %bitcast.30, f32[2,2,16,2,128]{4,3,2,1,0:T(2,128)} %bitcast.31, f32[8,2,128]{2,1,0:T(2,128)} %bitcast.33), custom_call_target="tpu_custom_call" | custom-call | tf_op jit(solution)/shard_map/pack/pallas_call | solution.py:338
  2.5 0.0 copy-start
  2.5 0.0 copy-start.1
  2.5 0.0 copy-start.2
  2.5 0.0 copy-start.3
  2.5 0.0 copy-start.4
  2.5 27.8 %all_to_all.20 = f32[16,81,2,128]{3,2,1,0:T(2,128)S(1)} all-to-all(f32[16,81,2,128]{3,2,1,0:T(2,128)S(1)} %bitcast.23), channel_id=1, replica_groups=mesh['micro'=8,'grid'=16] {'grid'}, dimensions={0} | all-to-all | bytes 2654208 | tf_op jit(solution)/shard_map/all_to_all | solution.py:353
  30.4 0.1 collective-permute-start
  30.5 0.0 copy-done
  30.5 0.0 copy-done.1
  30.5 0.0 copy-done.2
  30.5 0.0 copy-done.3
  30.5 0.0 copy-done.4
  30.5 1.4 %unpack.1 = (f32[2,16,4,16,128]{4,3,2,1,0:T(8,128)S(1)}, bf16[2,16,4,16,256]{4,3,2,1,0:T(8,128)(2,1)S(1)}, f32[16,4,16,128]{3,2,1,0:T(8,128)S(1)}, f32[40,128]{1,0:T(8,128)S(1)}, s32[64,128]{1,0:T(8,128)S(1)}) custom-call(s32[64]{0:T(128)S(1)} %copy-done.1, s32[64]{0:T(128)S(1)} %copy-done.3, s32[64]{0:T(128)S(1)} %copy-done.4, f32[2000]{0:T(1024)S(1)} %copy-done, ...), custom_call_target="tpu_custom_call" | custom-call | flops 10000000 | bytes 5242880 | tf_op jit(solution)/shard_map/unpack/pallas_call | solution.py:357
  31.9 0.1 collective-permute-done
  32.0 0.0 copy-start.5
  32.0 6.6 %first.1 = (f32[2,16,4,16,128]{4,3,2,1,0:T(8,128)S(1)}, bf16[16,4,16,384]{3,2,1,0:T(8,128)(2,1)S(1)}, bf16[256,1024]{1,0:T(8,128)(2,1)S(1)}, f32[128,128]{1,0:T(8,128)}) custom-call(f32[40,128]{1,0:T(8,128)S(1)} %get-tuple-element.13.small_ref, f32[2592,128]{1,0:T(8,128)S(1)} %bitcast.22, f32[512,128]{1,0:T(8,128)S(1)} %bitcast.26, ...), custom_call_target="tpu_custom_call" | custom-call | tf_op jit(solution)/shard_map/first/pallas_call | solution.py:379
  38.6 6.8 %all-to-all-start.1 = ((f32[128,1,128]{2,1,0:T(1,128)}), f32[128,1,128]{2,1,0:T(1,128)S(1)}, u32[]{:S(2)}, u32[]{:S(2)}) async-start(f32[128,1,128]{2,1,0:T(1,128)} %bitcast.7), calls=%async_computation.1 | async-start | bytes 131072 | tf_op jit(solution)/shard_map/all_to_all | solution.py:394
  45.4 0.0 copy-done.5
  45.4 9.2 %all-to-all-done.1 = f32[128,1,128]{2,1,0:T(1,128)S(1)} async-done(((f32[128,1,128]{2,1,0:T(1,128)}), f32[128,1,128]{2,1,0:T(1,128)S(1)}, u32[]{:S(2)}, u32[]{:S(2)}) %all-to-all-start.1) | async-done | bytes 65568 | tf_op jit(solution)/shard_map/all_to_all | solution.py:394
  54.6 5.7 %second.1 = (f32[2080,128]{1,0:T(8,128)S(1)}, f32[16,128]{1,0:T(8,128)S(1)}) custom-call(f32[40,128]{1,0:T(8,128)S(1)} %get-tuple-element.13.small_ref, s32[64,128]{1,0:T(8,128)S(1)} %get-tuple-element.14.cells_ref, f32[128,128]{1,0:T(8,128)S(1)} %bitcast.27, f32[16,128]{1,0:T(8,128)S(1)} %get-tuple-element.29.now_ref.old_ref, ...), custom_call_target="tpu_custom_call" | custom-call | tf_op jit(solution)/shard_map/second/pallas_call | solution.py:398
  60.4 21.4 %all_to_all.21 = f32[16,65,2,128]{3,2,1,0:T(2,128)S(1)} all-to-all(f32[16,65,2,128]{3,2,1,0:T(2,128)S(1)} %bitcast.25), channel_id=1, replica_groups=mesh['micro'=8,'grid'=16] {'grid'}, dimensions={0} | all-to-all | bytes 2129920 | tf_op jit(solution)/shard_map/all_to_all | solution.py:408
  81.8 0.6 broadcast_in_dim.3
  82.4 3.3 %all-to-all-start.3 = ((f32[8,8,128]{2,1,0:T(8,128)}), f32[8,8,128]{2,1,0:T(8,128)S(1)}, u32[]{:S(2)}, u32[]{:S(2)}) async-start(f32[8,8,128]{2,1,0:T(8,128)} %broadcast_in_dim.3), calls=%async_computation.3 | async-start | bytes 65536 | tf_op jit(solution)/shard_map/all_to_all | solution.py:410
  85.8 1.0 %unpermute.1 = f32[2,8,2,32,2,128]{5,4,3,2,1,0:T(2,128)} custom-call(f32[8,2,65,2,128]{4,3,2,1,0:T(2,128)S(1)} %bitcast.24), custom_call_target="tpu_custom_call" | custom-call | flops 1000000 | bytes 2097152 | tf_op jit(solution)/shard_map/unpermute/pallas_call | solution.py:411
  86.8 5.2 %all-to-all-done.3 = f32[8,8,128]{2,1,0:T(8,128)S(1)} async-done(((f32[8,8,128]{2,1,0:T(8,128)}), f32[8,8,128]{2,1,0:T(8,128)S(1)}, u32[]{:S(2)}, u32[]{:S(2)}) %all-to-all-start.3) | async-done | bytes 32800 | tf_op jit(solution)/shard_map/all_to_all | solution.py:410
  92.0 0.7 last.1
  (4 shorter events, 0.0 us)
Async XLA Ops:
  2.5 28.0 %copy-start = (f32[2000]{0:T(1024)S(1)}, f32[2000]{0:T(1024)}, u32[]{:S(2)}) copy-start(f32[2000]{0:T(1024)} %vector_ref.1) | copy-start | bytes 24004
  2.5 28.0 %copy-start.1 = (s32[64]{0:T(128)S(1)}, s32[64]{0:T(128)}, u32[]{:S(2)}) copy-start(s32[64]{0:T(128)} %kind_ref.1) | copy-start | bytes 772
  2.5 28.0 %copy-start.2 = (f32[2,32]{1,0:T(2,128)S(1)}, f32[2,32]{1,0:T(2,128)}, u32[]{:S(2)}) copy-start(f32[2,32]{1,0:T(2,128)} %strength_ref.1) | copy-start | bytes 772
  2.5 28.0 %copy-start.3 = (s32[64]{0:T(128)S(1)}, s32[64]{0:T(128)}, u32[]{:S(2)}) copy-start(s32[64]{0:T(128)} %cell_ref.1) | copy-start | bytes 772
  2.5 28.0 %copy-start.4 = (s32[64]{0:T(128)S(1)}, s32[64]{0:T(128)}, u32[]{:S(2)}) copy-start(s32[64]{0:T(128)} %material_ref.1) | copy-start | bytes 772
  30.4 1.6 %collective-permute-start = (f32[16,16,2,128]{3,2,1,0:T(2,128)S(1)}, f32[16,16,2,128]{3,2,1,0:T(2,128)S(1)}, u32[]{:S(2)}, u32[]{:S(2)}) collective-permute-start(f32[16,16,2,128]{3,2,1,0:T(2,128)S(1)} %slice.12), channel_id=1, source_target_pairs={{0,1},{1,0},{2,3},{3,2},{4,5},{5,4},{6,7},{7,6},{8,9},{9,8},{10,11... | collective-permute-start | bytes 786440 | tf_op jit(solution)/shard_map/ppermute | solution.py:354
  32.0 13.4 %copy-start.5 = (f32[2000]{0:T(1024)S(1)}, f32[2000]{0:T(1024)}, u32[]{:S(2)}) copy-start(f32[2000]{0:T(1024)} %param.17) | copy-start | bytes 24004
  38.6 16.0 %all-to-all-start.1 = ((f32[128,1,128]{2,1,0:T(1,128)}), f32[128,1,128]{2,1,0:T(1,128)S(1)}, u32[]{:S(2)}, u32[]{:S(2)}) async-start(f32[128,1,128]{2,1,0:T(1,128)} %bitcast.7), calls=%async_computation.1 | async-start | bytes 131072 | tf_op jit(solution)/shard_map/all_to_all | solution.py:394
  82.4 9.5 %all-to-all-start.3 = ((f32[8,8,128]{2,1,0:T(8,128)}), f32[8,8,128]{2,1,0:T(8,128)S(1)}, u32[]{:S(2)}, u32[]{:S(2)}) async-start(f32[8,8,128]{2,1,0:T(8,128)} %broadcast_in_dim.3), calls=%async_computation.3 | async-start | bytes 65536 | tf_op jit(solution)/shard_map/all_to_all | solution.py:410
